TPU v7x, 32 devices: a whole 2x2x4 slice. The times are simulated.
32 devices in a mesh: gx: 4 (over z), gy: 8 (over y, x, core).
Axes of the slice: x: 2, y: 2, z: 4, core: 2. Of those that a mesh axis runs over, the one named last changes fastest.
Arguments:
- saved_pops: bfloat16 [4, 19, 64, 4096], P(None, None, 'gx', 'gy'), may hold values from 0.099609375 to 1.8984375
- seed_adjoint: float32 [19, 64, 4096], P(None, 'gx', 'gy'), may hold values from -6 to 6
- solid_label: int32 [64, 4096], P('gx', 'gy'), may hold values 0 or 1
- design_mask: int32 [64, 4096], P('gx', 'gy'), may hold values 0 or 1
- design_field: float32 [64, 4096], P('gx', 'gy'), may hold values from 0 to 1
Outputs:
- adjoint_out: float32 [19, 64, 4096], P(None, 'gx', 'gy')
- sensitivity: float32 [64, 4096], P('gx', 'gy')
All inputs are finite; a program needn't handle non-finite values. No bound on the sum of `solid_label` or of `design_mask` on one device may be relied on, other than what follows from the above.
Results may differ from a plain program's by a relative error of at most 0.0003.
Values sent between devices are 32-bit elements; how exact they have to be, the bound alone decides.
A program may use at most 64 MiB of HBM per device.

v0:
```python
import jax
import jax.numpy as jnp
import numpy as np
from jax import lax
from jax.sharding import PartitionSpec as P

NZ = 32


VELOCITIES = np.array(
    [
        [0, 0, 0],
        [1, 0, 0],
        [-1, 0, 0],
        [0, 1, 0],
        [0, -1, 0],
        [0, 0, 1],
        [0, 0, -1],
        [1, 1, 0],
        [1, -1, 0],
        [-1, 1, 0],
        [-1, -1, 0],
        [1, 0, 1],
        [1, 0, -1],
        [-1, 0, 1],
        [-1, 0, -1],
        [0, 1, 1],
        [0, 1, -1],
        [0, -1, 1],
        [0, -1, -1],
    ]
)
LATTICE_WEIGHTS = np.array([1.0 / 3.0] + [1.0 / 18.0] * 6 + [1.0 / 36.0] * 12)
OPPOSITE = np.array([0, 2, 1, 4, 3, 6, 5, 10, 9, 8, 7, 14, 13, 12, 11, 18, 17, 16, 15])
OMEGA_BASE = 1.0
OMEGA_SPAN = 0.8
SENS_SCALE = 10.0


def extended(cells, sides, width):
    for axis, dim in sides:
        count = lax.axis_size(axis)
        head = lax.slice_in_dim(cells, 0, width, axis=dim)
        tail = lax.slice_in_dim(cells, cells.shape[dim] - width, cells.shape[dim], axis=dim)
        cells = jnp.concatenate(
            [
                lax.ppermute(tail, axis, [(i, (i + 1) % count) for i in range(count)]),
                cells,
                lax.ppermute(head, axis, [((i + 1) % count, i) for i in range(count)]),
            ],
            axis=dim,
        )
    return cells


def collide(pops, rates, solid):
    density = jnp.sum(pops, axis=0)
    velo = jnp.asarray(VELOCITIES, jnp.float32)
    momentum = jnp.tensordot(velo.T, pops, axes=1, precision=lax.Precision.HIGHEST)
    speed = momentum / density
    projected = jnp.tensordot(velo, speed, axes=1, precision=lax.Precision.HIGHEST)
    speed_sq = jnp.sum(speed * speed, axis=0)
    weights = jnp.asarray(LATTICE_WEIGHTS, jnp.float32).reshape((19,) + (1,) * (pops.ndim - 1))
    equilibrium = (
        weights * density * (1.0 + 3.0 * projected + 4.5 * projected * projected - 1.5 * speed_sq)
    )
    fluid = pops - rates * (pops - equilibrium)
    bounce = pops[OPPOSITE]
    return jnp.where(solid > 0, bounce, fluid)


def padded_field(field, depth):
    width, flat = (field.shape[1], field.shape[2])
    rows = flat // depth
    cube = field.reshape(19, width, rows, depth)
    padded = extended(cube, (("gx", 1), ("gy", 2)), 1)
    return padded.reshape(19, width + 2, (rows + 2) * depth)


def pull_back(field, depth):
    width, flat = (field.shape[1], field.shape[2])
    padded = padded_field(field, depth)
    depth_index = lax.broadcasted_iota(jnp.int32, (1, flat), 1) % depth
    planes = []
    for direction in range(19):
        step_x, step_y, step_z = (
            int(VELOCITIES[direction, 0]),
            int(VELOCITIES[direction, 1]),
            int(VELOCITIES[direction, 2]),
        )
        start = (1 + step_y) * depth
        window = padded[direction, 1 + step_x : 1 + step_x + width, start : start + flat]
        if step_z == 1:
            window = jnp.where(
                depth_index == depth - 1,
                jnp.roll(window, depth - 1, axis=1),
                jnp.roll(window, -1, axis=1),
            )
        elif step_z == -1:
            window = jnp.where(
                depth_index == 0, jnp.roll(window, 1 - depth, axis=1), jnp.roll(window, 1, axis=1)
            )
        planes.append(window)
    return jnp.stack(planes)


def body(saved_pops, seed_adjoint, solid_label, design_mask, design_field):
    num_steps = saved_pops.shape[0]
    width, flat = (seed_adjoint.shape[1], seed_adjoint.shape[2])
    mask_float = design_mask.astype(jnp.float32)
    rates = OMEGA_BASE + OMEGA_SPAN * design_field * mask_float
    weights = jnp.asarray(LATTICE_WEIGHTS, jnp.float32).reshape(19, 1, 1)
    adjoint = seed_adjoint
    sensitivity = jnp.zeros((width, flat), jnp.float32)

    def local(values, rate_values):
        return collide(values, rate_values, solid_label)

    for step in reversed(range(num_steps)):
        pulled = pull_back(adjoint, NZ)
        pops = saved_pops[step].astype(jnp.float32) * weights
        unused, backward = jax.vjp(local, pops, rates)
        adjoint, rate_bar = backward(pulled)
        sensitivity = sensitivity + SENS_SCALE * OMEGA_SPAN * mask_float * rate_bar
    return (adjoint, sensitivity)


def solution(mesh):
    in_specs = (
        P(None, None, "gx", "gy"),
        P(None, "gx", "gy"),
        P("gx", "gy"),
        P("gx", "gy"),
        P("gx", "gy"),
    )
    out_specs = (P(None, "gx", "gy"), P("gx", "gy"))
    return jax.shard_map(body, mesh=mesh, in_specs=in_specs, out_specs=out_specs, check_vma=False)
```

profile of v0, /device:TPU:0, one launch (start us, length us, event | category | flops | bytes accessed | tf_op | source)
XLA Modules:
  0.0 157.5 jit_solution(5921389567212766680)
XLA Ops:
  2.5 3.1 %collective-permute-start = (f32[19,1,16,32]{3,2,0,1:T(8,128)S(1)}, f32[19,1,16,32]{3,2,0,1:T(8,128)S(1)}, u32[]{:S(2)}, u32[]{:S(2)}) collective-permute-start(f32[19,1,16,32]{3,2,0,1:T(8,128)S(1)} %copy.519), channel_id=1, source_target_pairs={{0,8},{8,16},{16,24},{24,0},{1,9},{9,17},{17,25},{25,1},{2,10},{10... | collective-permute-start | bytes 116744 | tf_op jit(solution)/shard_map/ppermute | solution.py:47
  14.8 2.8 %collective-permute-start.3 = (f32[19,18,1,32]{3,2,0,1:T(1,128)S(1)}, f32[19,18,1,32]{3,2,0,1:T(1,128)S(1)}, u32[]{:S(2)}, u32[]{:S(2)}) collective-permute-start(f32[19,18,1,32]{3,2,0,1:T(1,128)S(1)} %get-tuple-element.26), channel_id=1, source_target_pairs={{1,0},{2,1},{3,2},{4,3},{5,4},{6,5},{7,6},{0,7},{9,8},{10,9},{11,1... | collective-permute-start | bytes 131336 | tf_op jit(solution)/shard_map/ppermute | solution.py:49
  17.6 3.0 %collective-permute-done.2 = f32[19,18,1,32]{3,2,0,1:T(1,128)S(1)} collective-permute-done((f32[19,18,1,32]{3,2,0,1:T(1,128)S(1)}, f32[19,18,1,32]{3,2,0,1:T(1,128)S(1)}, u32[]{:S(2)}, u32[]{:S(2)}) %collective-permute-start.2) | collective-permute-done | bytes 43808 | tf_op jit(solution)/shard_map/ppermute | solution.py:47
  20.5 2.8 %pad_maximum_fusion = f32[19,18,18,32]{3,2,0,1:T(8,128)} fusion(f32[19,18,1,32]{3,2,0,1:T(1,128)S(1)} %collective-permute-done.3, f32[19,18,16,32]{3,2,0,1:T(8,128)S(1)} %constant_dynamic-update-slice_fusion, f32[19,18,1,32]{3,2,0,1:T(1,128)S(1)} %collective-permute-done.2), kind=kLoop, calls=%fused_computation.4 | loop fusion | flops 393984 | bytes 1575936 | tf_op jit(solution)/shard_map/concatenate | solution.py:45
  23.3 3.2 %reshape.3200 = f32[19,18,576]{2,0,1:T(8,128)S(1)} reshape(f32[19,18,18,32]{3,2,0,1:T(8,128)} %pad_maximum_fusion) | data formatting | bytes 1575936 | tf_op jit(solution)/shard_map/reshape | solution.py:77
  44.8 2.8 %collective-permute-start.5 = (f32[19,1,16,32]{3,2,1,0:T(8,128)S(1)}, f32[19,1,16,32]{3,2,1,0:T(8,128)S(1)}, u32[]{:S(2)}, u32[]{:S(2)}) collective-permute-start(f32[19,1,16,32]{3,2,1,0:T(8,128)S(1)} %get-tuple-element.31), channel_id=1, source_target_pairs={{8,0},{16,8},{24,16},{0,24},{9,1},{17,9},{25,17},{1,25},{10,2},{18... | collective-permute-start | bytes 116744 | tf_op jit(solution)/shard_map/ppermute | solution.py:49
  49.0 3.7 %collective-permute-done.5 = f32[19,1,16,32]{3,2,1,0:T(8,128)S(1)} collective-permute-done((f32[19,1,16,32]{3,2,1,0:T(8,128)S(1)}, f32[19,1,16,32]{3,2,1,0:T(8,128)S(1)}, u32[]{:S(2)}, u32[]{:S(2)}) %collective-permute-start.5) | collective-permute-done | bytes 38944 | tf_op jit(solution)/shard_map/ppermute | solution.py:49
  55.7 4.0 %collective-permute-done.6 = f32[19,18,1,32]{3,2,1,0:T(1,128)S(1)} collective-permute-done((f32[19,18,1,32]{3,2,1,0:T(1,128)S(1)}, f32[19,18,1,32]{3,2,1,0:T(1,128)S(1)}, u32[]{:S(2)}, u32[]{:S(2)}) %collective-permute-start.6) | collective-permute-done | bytes 43808 | tf_op jit(solution)/shard_map/ppermute | solution.py:47
  59.8 2.8 %pad_maximum_fusion.1 = f32[19,18,18,32]{3,2,1,0:T(8,128)} fusion(f32[19,18,1,32]{3,2,1,0:T(1,128)S(1)} %collective-permute-done.7, f32[19,18,16,32]{3,2,1,0:T(8,128)S(1)} %constant_dynamic-update-slice_fusion.3, f32[19,18,1,32]{3,2,1,0:T(1,128)S(1)} %collective-permute-done.6), kind=kLoop, calls=%fused_computation.5 | loop fusion | flops 393984 | bytes 1575936 | tf_op jit(solution)/shard_map/concatenate | solution.py:45
  62.6 3.2 %reshape.3244 = f32[19,18,576]{2,1,0:T(8,128)S(1)} reshape(f32[19,18,18,32]{3,2,1,0:T(8,128)} %pad_maximum_fusion.1) | data formatting | bytes 1575936 | tf_op jit(solution)/shard_map/reshape | solution.py:77
  71.0 2.9 %fusion.14 = (f32[16,512]{1,0:T(8,128)}, f32[16,512]{1,0:T(8,128)S(1)}, f32[16,512]{1,0:T(8,128)S(1)}, f32[16,512]{1,0:T(8,128)S(1)}, f32[16,512]{1,0:T(8,128)},...) fusion(f32[19,16,512]{2,0,1:T(8,128)S(1)} %stack.9, f32[16,512]{1,0:T(8,128)S(1)} %broadcast_multiply_fusion.2, ...), kind=kOutput, calls=%fused_computation.45 | convolution fusion | flops 10100736 | bytes 3170608 | tf_op jit(solution)/shard_map/jvp()/dot_general | solution.py:61
  82.6 2.6 %multiply_reduce_fusion.5 = (f32[16,512]{1,0:T(8,128)}, f32[3,16,512]{2,0,1:T(4,128)}) fusion(f32[16,512]{1,0:T(8,128)S(1)} %get-tuple-element.16, f32[19,3,1]{0,1,2:T(4,128)} %constant.69, f32[19]{0:T(128)} %constant.60.clone, bf16[1,19,16,512]{3,2,1,0:T(8,128)(2,1)S(1)} %get-tuple-element.38), kind=kOutput, calls=%fused_computation.145 | convolution fusion | flops 5980160 | bytes 475440 | tf_op jit(solution)/shard_map/jvp()/dot_general | solution.py:59
  85.8 3.3 %collective-permute-start.9 = (f32[19,1,16,32]{3,2,1,0:T(8,128)S(1)}, f32[19,1,16,32]{3,2,1,0:T(8,128)S(1)}, u32[]{:S(2)}, u32[]{:S(2)}) collective-permute-start(f32[19,1,16,32]{3,2,1,0:T(8,128)S(1)} %get-tuple-element.29), channel_id=1, source_target_pairs={{8,0},{16,8},{24,16},{0,24},{9,1},{17,9},{25,17},{1,25},{10,2},{18... | collective-permute-start | bytes 116744 | tf_op jit(solution)/shard_map/ppermute | solution.py:49
  89.4 3.8 %collective-permute-done.9 = f32[19,1,16,32]{3,2,1,0:T(8,128)S(1)} collective-permute-done((f32[19,1,16,32]{3,2,1,0:T(8,128)S(1)}, f32[19,1,16,32]{3,2,1,0:T(8,128)S(1)}, u32[]{:S(2)}, u32[]{:S(2)}) %collective-permute-start.9) | collective-permute-done | bytes 38944 | tf_op jit(solution)/shard_map/ppermute | solution.py:49
  96.1 4.8 %collective-permute-done.10 = f32[19,18,1,32]{3,2,1,0:T(1,128)S(1)} collective-permute-done((f32[19,18,1,32]{3,2,1,0:T(1,128)S(1)}, f32[19,18,1,32]{3,2,1,0:T(1,128)S(1)}, u32[]{:S(2)}, u32[]{:S(2)}) %collective-permute-start.10) | collective-permute-done | bytes 43808 | tf_op jit(solution)/shard_map/ppermute | solution.py:47
  100.9 2.8 %pad_maximum_fusion.2 = f32[19,18,18,32]{3,2,1,0:T(8,128)} fusion(f32[19,18,1,32]{3,2,1,0:T(1,128)S(1)} %collective-permute-done.11, f32[19,18,16,32]{3,2,1,0:T(8,128)S(1)} %constant_dynamic-update-slice_fusion.6, f32[19,18,1,32]{3,2,1,0:T(1,128)S(1)} %collective-permute-done.10), kind=kLoop, calls=%fused_computation.6 | loop fusion | flops 393984 | bytes 1575936 | tf_op jit(solution)/shard_map/concatenate | solution.py:45
  103.8 3.2 %reshape.3245 = f32[19,18,576]{2,1,0:T(8,128)S(1)} reshape(f32[19,18,18,32]{3,2,1,0:T(8,128)} %pad_maximum_fusion.2) | data formatting | bytes 1575936 | tf_op jit(solution)/shard_map/reshape | solution.py:77
  121.2 3.7 %collective-permute-start.13 = (f32[19,1,16,32]{3,2,1,0:T(8,128)S(1)}, f32[19,1,16,32]{3,2,1,0:T(8,128)S(1)}, u32[]{:S(2)}, u32[]{:S(2)}) collective-permute-start(f32[19,1,16,32]{3,2,1,0:T(8,128)S(1)} %get-tuple-element.27), channel_id=1, source_target_pairs={{8,0},{16,8},{24,16},{0,24},{9,1},{17,9},{25,17},{1,25},{10,2},{18... | collective-permute-start | bytes 116744 | tf_op jit(solution)/shard_map/ppermute | solution.py:49
  125.0 4.3 %collective-permute-done.12 = f32[19,1,16,32]{3,2,1,0:T(8,128)S(1)} collective-permute-done((f32[19,1,16,32]{3,2,1,0:T(8,128)S(1)}, f32[19,1,16,32]{3,2,1,0:T(8,128)S(1)}, u32[]{:S(2)}, u32[]{:S(2)}) %collective-permute-start.12) | collective-permute-done | bytes 38944 | tf_op jit(solution)/shard_map/ppermute | solution.py:47
  130.7 2.8 %collective-permute-start.15 = (f32[19,18,1,32]{3,2,1,0:T(1,128)S(1)}, f32[19,18,1,32]{3,2,1,0:T(1,128)S(1)}, u32[]{:S(2)}, u32[]{:S(2)}) collective-permute-start(f32[19,18,1,32]{3,2,1,0:T(1,128)S(1)} %get-tuple-element.20), channel_id=1, source_target_pairs={{1,0},{2,1},{3,2},{4,3},{5,4},{6,5},{7,6},{0,7},{9,8},{10,9},{11,1... | collective-permute-start | bytes 131336 | tf_op jit(solution)/shard_map/ppermute | solution.py:49
  133.6 4.1 %collective-permute-done.14 = f32[19,18,1,32]{3,2,1,0:T(1,128)S(1)} collective-permute-done((f32[19,18,1,32]{3,2,1,0:T(1,128)S(1)}, f32[19,18,1,32]{3,2,1,0:T(1,128)S(1)}, u32[]{:S(2)}, u32[]{:S(2)}) %collective-permute-start.14) | collective-permute-done | bytes 43808 | tf_op jit(solution)/shard_map/ppermute | solution.py:47
  137.7 2.8 %pad_maximum_fusion.3 = f32[19,18,18,32]{3,2,1,0:T(8,128)} fusion(f32[19,18,1,32]{3,2,1,0:T(1,128)S(1)} %collective-permute-done.15, f32[19,18,16,32]{3,2,1,0:T(8,128)S(1)} %constant_dynamic-update-slice_fusion.9, f32[19,18,1,32]{3,2,1,0:T(1,128)S(1)} %collective-permute-done.14), kind=kLoop, calls=%fused_computation.7 | loop fusion | flops 393984 | bytes 1575936 | tf_op jit(solution)/shard_map/concatenate | solution.py:45
  140.5 3.2 %reshape.3246 = f32[19,18,576]{2,1,0:T(8,128)S(1)} reshape(f32[19,18,18,32]{3,2,1,0:T(8,128)} %pad_maximum_fusion.3) | data formatting | bytes 1575936 | tf_op jit(solution)/shard_map/reshape | solution.py:77
  148.8 2.7 %fusion.30 = (f32[16,512]{1,0:T(8,128)S(1)}, f32[16,512]{1,0:T(8,128)S(1)}, f32[16,512]{1,0:T(8,128)S(1)}, f32[19,16,512]{2,0,1:T(8,128)S(1)}, f32[19,16,512]{2,0,1:T(8,128)S(1)}) fusion(f32[19,16,512]{2,0,1:T(8,128)S(1)} %stack.11, f32[16,512]{1,0:T(8,128)S(1)} %broadcast_multiply_fusion, f32[16,512]{1,0:T(8,128)S(1)} %get-tuple-element.16, ...), kind=kOutput, calls=%fused_computation.59 | convolution fusion | flops 9183232 | bytes 2482480 | tf_op jit(solution)/shard_map/jvp()/dot_general | solution.py:61
  (466 shorter events, 76.2 us)
Async XLA Ops:
  0.6 9.1 %copy-start.36 = (f32[19]{0:T(128)S(1)}, f32[19]{0:T(128)}, u32[]{:S(2)}) copy-start(f32[19]{0:T(128)} %constant.60.clone) | copy-start | bytes 232
  2.4 8.3 %copy-start.42 = (f32[19,3,1]{0,1,2:T(4,128)S(1)}, f32[19,3,1]{0,1,2:T(4,128)}, u32[]{:S(2)}) copy-start(f32[19,3,1]{0,1,2:T(4,128)} %constant.69) | copy-start | bytes 688
  2.4 9.6 %copy-start.7 = (s32[16,512]{1,0:T(8,128)S(1)}, s32[16,512]{1,0:T(8,128)}, u32[]{:S(2)}) copy-start(s32[16,512]{1,0:T(8,128)} %param.21) | copy-start | bytes 98308
  2.4 10.2 %copy-start.5 = (s32[16,512]{1,0:T(8,128)S(1)}, s32[16,512]{1,0:T(8,128)}, u32[]{:S(2)}) copy-start(s32[16,512]{1,0:T(8,128)} %param.22) | copy-start | bytes 98308
  2.4 10.2 %copy-start.6 = (f32[16,512]{1,0:T(8,128)S(1)}, f32[16,512]{1,0:T(8,128)}, u32[]{:S(2)}) copy-start(f32[16,512]{1,0:T(8,128)} %param.23) | copy-start | bytes 98308
  2.5 10.8 %collective-permute-start = (f32[19,1,16,32]{3,2,0,1:T(8,128)S(1)}, f32[19,1,16,32]{3,2,0,1:T(8,128)S(1)}, u32[]{:S(2)}, u32[]{:S(2)}) collective-permute-start(f32[19,1,16,32]{3,2,0,1:T(8,128)S(1)} %copy.519), channel_id=1, source_target_pairs={{0,8},{8,16},{16,24},{24,0},{1,9},{9,17},{17,25},{25,1},{2,10},{10... | collective-permute-start | bytes 116744 | tf_op jit(solution)/shard_map/ppermute | solution.py:47
  5.6 8.9 %collective-permute-start.1 = (f32[19,1,16,32]{3,2,0,1:T(8,128)S(1)}, f32[19,1,16,32]{3,2,0,1:T(8,128)S(1)}, u32[]{:S(2)}, u32[]{:S(2)}) collective-permute-start(f32[19,1,16,32]{3,2,0,1:T(8,128)S(1)} %copy.520), channel_id=1, source_target_pairs={{8,0},{16,8},{24,16},{0,24},{9,1},{17,9},{25,17},{1,25},{10,2},{18... | collective-permute-start | bytes 116744 | tf_op jit(solution)/shard_map/ppermute | solution.py:49
  9.7 22.4 %copy-start.3 = (bf16[1,19,16,512]{3,2,1,0:T(8,128)(2,1)}, bf16[1,19,16,512]{3,2,1,0:T(8,128)(2,1)S(1)}, u32[]{:S(2)}) copy-start(bf16[1,19,16,512]{3,2,1,0:T(8,128)(2,1)S(1)} %get-tuple-element.36) | copy-start | bytes 933892
  14.7 5.8 %collective-permute-start.2 = (f32[19,18,1,32]{3,2,0,1:T(1,128)S(1)}, f32[19,18,1,32]{3,2,0,1:T(1,128)S(1)}, u32[]{:S(2)}, u32[]{:S(2)}) collective-permute-start(f32[19,18,1,32]{3,2,0,1:T(1,128)S(1)} %get-tuple-element.25), channel_id=1, source_target_pairs={{0,1},{1,2},{2,3},{3,4},{4,5},{5,6},{6,7},{7,0},{8,9},{9,10},{10,1... | collective-permute-start | bytes 131336 | tf_op jit(solution)/shard_map/ppermute | solution.py:47
  14.8 5.8 %collective-permute-start.3 = (f32[19,18,1,32]{3,2,0,1:T(1,128)S(1)}, f32[19,18,1,32]{3,2,0,1:T(1,128)S(1)}, u32[]{:S(2)}, u32[]{:S(2)}) collective-permute-start(f32[19,18,1,32]{3,2,0,1:T(1,128)S(1)} %get-tuple-element.26), channel_id=1, source_target_pairs={{1,0},{2,1},{3,2},{4,3},{5,4},{6,5},{7,6},{0,7},{9,8},{10,9},{11,1... | collective-permute-start | bytes 131336 | tf_op jit(solution)/shard_map/ppermute | solution.py:49
  17.6 13.3 %copy-start.24 = (pred[512]{0:T(512)(128)(4,1)}, pred[512]{0:T(512)(128)(4,1)S(1)}, u32[]{:S(2)}) copy-start(pred[512]{0:T(512)(128)(4,1)S(1)} %fusion.103) | copy-start | bytes 1540
  40.3 8.4 %collective-permute-start.4 = (f32[19,1,16,32]{3,2,1,0:T(8,128)S(1)}, f32[19,1,16,32]{3,2,1,0:T(8,128)S(1)}, u32[]{:S(2)}, u32[]{:S(2)}) collective-permute-start(f32[19,1,16,32]{3,2,1,0:T(8,128)S(1)} %get-tuple-element.32), channel_id=1, source_target_pairs={{0,8},{8,16},{16,24},{24,0},{1,9},{9,17},{17,25},{25,1},{2,10},{10... | collective-permute-start | bytes 116744 | tf_op jit(solution)/shard_map/ppermute | solution.py:47
  44.8 8.0 %collective-permute-start.5 = (f32[19,1,16,32]{3,2,1,0:T(8,128)S(1)}, f32[19,1,16,32]{3,2,1,0:T(8,128)S(1)}, u32[]{:S(2)}, u32[]{:S(2)}) collective-permute-start(f32[19,1,16,32]{3,2,1,0:T(8,128)S(1)} %get-tuple-element.31), channel_id=1, source_target_pairs={{8,0},{16,8},{24,16},{0,24},{9,1},{17,9},{25,17},{1,25},{10,2},{18... | collective-permute-start | bytes 116744 | tf_op jit(solution)/shard_map/ppermute | solution.py:49
  53.0 6.7 %collective-permute-start.6 = (f32[19,18,1,32]{3,2,1,0:T(1,128)S(1)}, f32[19,18,1,32]{3,2,1,0:T(1,128)S(1)}, u32[]{:S(2)}, u32[]{:S(2)}) collective-permute-start(f32[19,18,1,32]{3,2,1,0:T(1,128)S(1)} %get-tuple-element.23), channel_id=1, source_target_pairs={{0,1},{1,2},{2,3},{3,4},{4,5},{5,6},{6,7},{7,0},{8,9},{9,10},{10,1... | collective-permute-start | bytes 131336 | tf_op jit(solution)/shard_map/ppermute | solution.py:47
  53.2 6.6 %collective-permute-start.7 = (f32[19,18,1,32]{3,2,1,0:T(1,128)S(1)}, f32[19,18,1,32]{3,2,1,0:T(1,128)S(1)}, u32[]{:S(2)}, u32[]{:S(2)}) collective-permute-start(f32[19,18,1,32]{3,2,1,0:T(1,128)S(1)} %get-tuple-element.24), channel_id=1, source_target_pairs={{1,0},{2,1},{3,2},{4,3},{5,4},{6,5},{7,6},{0,7},{9,8},{10,9},{11,1... | collective-permute-start | bytes 131336 | tf_op jit(solution)/shard_map/ppermute | solution.py:49
  66.3 4.6 %copy-start.4 = (bf16[1,19,16,512]{3,2,1,0:T(8,128)(2,1)S(1)}, bf16[1,19,16,512]{3,2,1,0:T(8,128)(2,1)}, u32[]{:S(2)}) copy-start(bf16[1,19,16,512]{3,2,1,0:T(8,128)(2,1)} %copy-done.3) | copy-start | bytes 933892
  79.4 9.7 %collective-permute-start.8 = (f32[19,1,16,32]{3,2,1,0:T(8,128)S(1)}, f32[19,1,16,32]{3,2,1,0:T(8,128)S(1)}, u32[]{:S(2)}, u32[]{:S(2)}) collective-permute-start(f32[19,1,16,32]{3,2,1,0:T(8,128)S(1)} %get-tuple-element.30), channel_id=1, source_target_pairs={{0,8},{8,16},{16,24},{24,0},{1,9},{9,17},{17,25},{25,1},{2,10},{10... | collective-permute-start | bytes 116744 | tf_op jit(solution)/shard_map/ppermute | solution.py:47
  85.8 7.3 %collective-permute-start.9 = (f32[19,1,16,32]{3,2,1,0:T(8,128)S(1)}, f32[19,1,16,32]{3,2,1,0:T(8,128)S(1)}, u32[]{:S(2)}, u32[]{:S(2)}) collective-permute-start(f32[19,1,16,32]{3,2,1,0:T(8,128)S(1)} %get-tuple-element.29), channel_id=1, source_target_pairs={{8,0},{16,8},{24,16},{0,24},{9,1},{17,9},{25,17},{1,25},{10,2},{18... | collective-permute-start | bytes 116744 | tf_op jit(solution)/shard_map/ppermute | solution.py:49
  93.4 7.5 %collective-permute-start.10 = (f32[19,18,1,32]{3,2,1,0:T(1,128)S(1)}, f32[19,18,1,32]{3,2,1,0:T(1,128)S(1)}, u32[]{:S(2)}, u32[]{:S(2)}) collective-permute-start(f32[19,18,1,32]{3,2,1,0:T(1,128)S(1)} %get-tuple-element.21), channel_id=1, source_target_pairs={{0,1},{1,2},{2,3},{3,4},{4,5},{5,6},{6,7},{7,0},{8,9},{9,10},{10,1... | collective-permute-start | bytes 131336 | tf_op jit(solution)/shard_map/ppermute | solution.py:47
  93.5 7.4 %collective-permute-start.11 = (f32[19,18,1,32]{3,2,1,0:T(1,128)S(1)}, f32[19,18,1,32]{3,2,1,0:T(1,128)S(1)}, u32[]{:S(2)}, u32[]{:S(2)}) collective-permute-start(f32[19,18,1,32]{3,2,1,0:T(1,128)S(1)} %get-tuple-element.22), channel_id=1, source_target_pairs={{1,0},{2,1},{3,2},{4,3},{5,4},{6,5},{7,6},{0,7},{9,8},{10,9},{11,1... | collective-permute-start | bytes 131336 | tf_op jit(solution)/shard_map/ppermute | solution.py:49
  120.0 9.2 %collective-permute-start.12 = (f32[19,1,16,32]{3,2,1,0:T(8,128)S(1)}, f32[19,1,16,32]{3,2,1,0:T(8,128)S(1)}, u32[]{:S(2)}, u32[]{:S(2)}) collective-permute-start(f32[19,1,16,32]{3,2,1,0:T(8,128)S(1)} %get-tuple-element.28), channel_id=1, source_target_pairs={{0,8},{8,16},{16,24},{24,0},{1,9},{9,17},{17,25},{25,1},{2,10},{10... | collective-permute-start | bytes 116744 | tf_op jit(solution)/shard_map/ppermute | solution.py:47
  121.2 9.2 %collective-permute-start.13 = (f32[19,1,16,32]{3,2,1,0:T(8,128)S(1)}, f32[19,1,16,32]{3,2,1,0:T(8,128)S(1)}, u32[]{:S(2)}, u32[]{:S(2)}) collective-permute-start(f32[19,1,16,32]{3,2,1,0:T(8,128)S(1)} %get-tuple-element.27), channel_id=1, source_target_pairs={{8,0},{16,8},{24,16},{0,24},{9,1},{17,9},{25,17},{1,25},{10,2},{18... | collective-permute-start | bytes 116744 | tf_op jit(solution)/shard_map/ppermute | solution.py:49
  130.7 7.0 %collective-permute-start.14 = (f32[19,18,1,32]{3,2,1,0:T(1,128)S(1)}, f32[19,18,1,32]{3,2,1,0:T(1,128)S(1)}, u32[]{:S(2)}, u32[]{:S(2)}) collective-permute-start(f32[19,18,1,32]{3,2,1,0:T(1,128)S(1)} %get-tuple-element.19), channel_id=1, source_target_pairs={{0,1},{1,2},{2,3},{3,4},{4,5},{5,6},{6,7},{7,0},{8,9},{9,10},{10,1... | collective-permute-start | bytes 131336 | tf_op jit(solution)/shard_map/ppermute | solution.py:47
  130.7 6.9 %collective-permute-start.15 = (f32[19,18,1,32]{3,2,1,0:T(1,128)S(1)}, f32[19,18,1,32]{3,2,1,0:T(1,128)S(1)}, u32[]{:S(2)}, u32[]{:S(2)}) collective-permute-start(f32[19,18,1,32]{3,2,1,0:T(1,128)S(1)} %get-tuple-element.20), channel_id=1, source_target_pairs={{1,0},{2,1},{3,2},{4,3},{5,4},{6,5},{7,6},{0,7},{9,8},{10,9},{11,1... | collective-permute-start | bytes 131336 | tf_op jit(solution)/shard_map/ppermute | solution.py:49
  (45 other events, 164.9 us)
where the time goes:
time: 161 us; the launch traced here: 157 us
  local copies, waits for them, and re-layouts  37.4 us (23%)
  waiting for transfers between devices  30.8 us (19%)
  other arithmetic  30.5 us (19%)
  starting transfers between devices  29 us (18%)
  matrix products  27 us (17%)
  between operations  2.8 us (2%)
    ppermute x8, starting transfers between devices, extended(): lax.ppermute(head, axis, [((i + 1) % count, i) for i in range(count)])  22.6 us
    ppermute x8, waiting for transfers between devices, extended(): lax.ppermute(tail, axis, [(i, (i + 1) % count) for i in range(count)])  21.3 us
    dot_general x8, matrix products, collide(): jnp.tensordot(velo, speed, axes=1, precision=lax.Precision.HIGHEST)  14.4 us
    reshape x4, local copies, waits for them, and re-layouts, padded_field(): return padded.reshape(19, width + 2, (rows + 2) * depth)  12.9 us
    dot_general x8, matrix products, collide(): jnp.tensordot(velo.T, pops, axes=1, precision=lax.Precision.HIGHEST)  12.6 us
    concatenate x4, other arithmetic, extended(): jnp.concatenate([lax.ppermute(tail, axis, [(i, (i + 1) % count) for i in...  11.3 us
    ppermute x8, waiting for transfers between devices, extended(): lax.ppermute(head, axis, [((i + 1) % count, i) for i in range(count)])  9.48 us
    scatter-add x4, other arithmetic, collide(): bounce = pops[OPPOSITE]  8.51 us
  transfers between devices with their start and end apart: 16, of which 10 were waited for; matrix products, arithmetic and copies ran while one was open for 10% of the time, Pallas kernels for 0%

commit v1 on v0

v1 whole, which is shorter than its diff:
```python
import functools

import jax
import jax.numpy as jnp
import numpy as np
from jax import lax
from jax.experimental import pallas as pl
from jax.experimental.pallas import tpu as pltpu
from jax.sharding import PartitionSpec as P

NZ = 32
LANES = 128
MESH = pl.DeviceIdType.MESH

VELOCITIES = [
    (0, 0, 0),
    (1, 0, 0), (-1, 0, 0), (0, 1, 0), (0, -1, 0), (0, 0, 1), (0, 0, -1),
    (1, 1, 0), (1, -1, 0), (-1, 1, 0), (-1, -1, 0),
    (1, 0, 1), (1, 0, -1), (-1, 0, 1), (-1, 0, -1),
    (0, 1, 1), (0, 1, -1), (0, -1, 1), (0, -1, -1),
]
OPPOSITE = [0, 2, 1, 4, 3, 6, 5, 10, 9, 8, 7, 14, 13, 12, 11, 18, 17, 16, 15]
OMEGA_BASE = 1.0
OMEGA_SPAN = 0.8
SENS_SCALE = 10.0

ORDER = [1, 7, 8, 11, 12, 2, 9, 10, 13, 14, 0, 3, 4, 5, 6, 15, 16, 17, 18]
PLACE = [ORDER.index(k) for k in range(19)]
PACKED = {
    3: (0, 0, 0), 7: (0, 0, 1), 9: (0, 0, 2), 15: (0, 0, 3), 16: (0, 1, 0),
    4: (1, 0, 3), 8: (1, 0, 2), 10: (1, 0, 1), 17: (1, 0, 0), 18: (1, 1, 3),
}
TOP = 8


def roll_lanes(value, shift):
    shift = shift % LANES
    return value if shift == 0 else pltpu.roll(value, shift, 1)


def kernel(
    num_x, num_y, steps, width, flat,
    saved_hbm, seed_hbm, solid_hbm, mask_hbm, field_hbm,
    out_hbm, sens_hbm,
    saved, seed, solid_ref, mask_ref, field_ref,
    adj, ysend, yrecv, flow, rate_ref, out, sens,
    in_sem, saved_sem, out_sem, send_sem, recv_sem,
):
    tiles = flat // LANES
    gx, gy = lax.axis_index("gx"), lax.axis_index("gy")
    west, east = lax.rem(gx + num_x - 1, num_x), lax.rem(gx + 1, num_x)
    south, north = lax.rem(gy + num_y - 1, num_y), lax.rem(gy + 1, num_y)

    barrier = pltpu.get_barrier_semaphore()
    around = [
        (west, gy), (east, gy), (gx, south), (gx, north),
        (west, south), (east, south), (west, north), (east, north),
    ]
    loads = [
        pltpu.make_async_copy(seed_hbm, seed, in_sem.at[0]),
        pltpu.make_async_copy(solid_hbm, solid_ref, in_sem.at[1]),
        pltpu.make_async_copy(mask_hbm, mask_ref, in_sem.at[2]),
        pltpu.make_async_copy(field_hbm, field_ref, in_sem.at[3]),
    ]
    saved_loads = [
        pltpu.make_async_copy(saved_hbm.at[s], saved.at[s], saved_sem.at[s]) for s in range(steps)
    ]
    loads[0].start()
    for device in around:
        pl.semaphore_signal(barrier, inc=1, device_id=device, device_id_type=MESH)
    for load in loads[1:]:
        load.start()
    for s in reversed(range(steps)):
        saved_loads[s].start()

    lane = lax.broadcasted_iota(jnp.int32, (width, LANES), 1)
    depth = lane % NZ
    own = pl.ds(TOP, width)

    def transfers(n):
        moves = []

        def add(src, dst, device):
            i = len(moves)
            moves.append(
                pltpu.make_async_remote_copy(
                    src_ref=src, dst_ref=dst,
                    send_sem=send_sem.at[n, i], recv_sem=recv_sem.at[n, i],
                    device_id=device, device_id_type=MESH,
                )
            )

        rows = {1: (TOP, TOP + width), -1: (TOP + width - 1, TOP - 1)}
        for first, step_x, device in ((0, 1, (west, gy)), (5, -1, (east, gy))):
            src_row, dst_row = rows[step_x]
            group = adj.at[n, pl.ds(first, 5)]
            add(group.at[:, :, pl.ds(src_row, 1)], group.at[:, :, pl.ds(dst_row, 1)], device)
        for side, device in ((0, (gx, south)), (1, (gx, north))):
            add(ysend.at[n, side, :, own], yrecv.at[n, side, :, own], device)
        for side, step_x, device in (
            (0, 1, (west, south)), (0, -1, (east, south)), (1, 1, (west, north)), (1, -1, (east, north)),
        ):
            src_row, dst_row = rows[step_x]
            add(
                ysend.at[n, side, 0, pl.ds(src_row, 1)],
                yrecv.at[n, side, 0, pl.ds(dst_row, 1)],
                device,
            )
        return moves

    def pack(n, side, value):
        blocks, extra = [None] * 4, None
        for k, (where, tile, block) in PACKED.items():
            if where != side:
                continue
            if tile == 1:
                extra = value(k)
            else:
                blocks[block] = roll_lanes(value(k), NZ * (block - (0 if side == 0 else 3)))
        low = jnp.where(lane < NZ, blocks[0], blocks[1])
        high = jnp.where(lane < 3 * NZ, blocks[2], blocks[3])
        ysend[n, side, 0, own, :] = jnp.where(lane < 2 * NZ, low, high)
        ysend[n, side, 1, own, :] = extra

    def pulled_tile(n, k, t):
        step_x, step_y, step_z = VELOCITIES[k]
        rows = pl.ds(TOP + step_x, width)
        value = adj[n, PLACE[k], t, rows, :]
        if step_y != 0:
            other = t + step_y
            if 0 <= other < tiles:
                beside = adj[n, PLACE[k], other, rows, :]
            else:
                side, tile, block = PACKED[k]
                beside = roll_lanes(
                    yrecv[n, side, tile, rows, :], NZ * ((0 if side == 0 else 3) - block)
                )
            edge = lane < NZ if step_y == 1 else lane >= LANES - NZ
            value = jnp.where(edge, beside, value)
        shift = -NZ * step_y
        if step_z == 0:
            return roll_lanes(value, shift)
        wraps = depth == (NZ - 1 if step_z == 1 else 0)
        return jnp.where(
            wraps,
            roll_lanes(value, shift - step_z + NZ * step_z),
            roll_lanes(value, shift - step_z),
        )

    def moments(v):
        xy_a, xy_b, xy_c, xy_d = v(7) + v(8), v(9) + v(10), v(7) - v(8), v(9) - v(10)
        xz_a, xz_b, xz_c, xz_d = v(11) + v(12), v(13) + v(14), v(11) - v(12), v(13) - v(14)
        yz_a, yz_b, yz_c, yz_d = v(15) + v(16), v(17) + v(18), v(15) - v(16), v(17) - v(18)
        xy, xz, yz = xy_a + xy_b, xz_a + xz_b, yz_a + yz_b
        face_x, face_y, face_z = 2.0 * (v(1) + v(2)), 2.0 * (v(3) + v(4)), 2.0 * (v(5) + v(6))
        total = 12.0 * v(0) + (face_x + face_y + face_z) + (xy + xz + yz)
        first = (
            2.0 * (v(1) - v(2)) + (xy_a - xy_b) + (xz_a - xz_b),
            2.0 * (v(3) - v(4)) + (xy_c + xy_d) + (yz_a - yz_b),
            2.0 * (v(5) - v(6)) + (xz_c + xz_d) + (yz_c + yz_d),
        )
        second = (
            face_x + xy + xz, face_y + xy + yz, face_z + xz + yz,
            xy_c - xy_d, xz_c - xz_d, yz_c - yz_d,
        )
        return total, first, second

    def prepare(s):
        for t in range(tiles):
            cols = pl.ds(t * LANES, LANES)
            pops = [saved[s, k, :, cols].astype(jnp.float32) for k in range(19)]
            total, first, unused = moments(lambda k: pops[k])
            inverse = 1.0 / total
            flow[s, 0, t] = total
            for axis in range(3):
                flow[s, 1 + axis, t] = first[axis] * inverse

    def advance(n, t, emit):
        s = steps - 1 - n
        cols = pl.ds(t * LANES, LANES)
        p = [pulled_tile(n, k, t) for k in range(19)]
        total, first, second = moments(lambda k: p[k])
        density, ux, uy, uz = (flow[s, i, t] for i in range(4))
        xx, yy, zz, xy, xz, yz = (0.25 * value for value in second)
        gx_, gy_, gz_ = (value * (1.0 / 12.0) for value in first)
        total3 = total * (1.0 / 12.0)
        dx = gx_ + (xx - total3) * ux + xy * uy + xz * uz
        dy = gy_ + (yy - total3) * uy + xy * ux + yz * uz
        dz = gz_ + (zz - total3) * uz + xz * ux + yz * uy
        half_g = 0.5 * (gx_ * ux + gy_ * uy + gz_ * uz)
        half_d = 0.5 * (dx * ux + dy * uy + dz * uz)
        base = total * (1.0 / 36.0) + half_g
        prod = [p[k] * saved[s, k, :, cols].astype(jnp.float32) for k in range(19)]
        faces = (prod[1] + prod[2]) + (prod[3] + prod[4]) + (prod[5] + prod[6])
        edges = ((prod[7] + prod[8]) + (prod[9] + prod[10])) + ((prod[11] + prod[12]) + (prod[13] + prod[14]))
        edges = edges + ((prod[15] + prod[16]) + (prod[17] + prod[18]))
        gain = density * (base + half_d) - (12.0 * prod[0] + 2.0 * faces + edges)
        sens_now = gain if n == 0 else sens[:, cols] + gain
        solid = solid_ref[:, cols] > 0
        if n == steps - 1:
            factor = mask_ref[:, cols].astype(jnp.float32) * (SENS_SCALE * OMEGA_SPAN / 36.0)
            sens_now = jnp.where(solid, 0.0, factor * sens_now)
        sens[:, cols] = sens_now
        rate = rate_ref[:, cols]
        keep = 1.0 - rate
        base = rate * (base - half_d)
        dx, dy, dz = rate * dx, rate * dy, rate * dz
        px, mx = base + dx, base - dx
        py, my = base + dy, base - dy
        terms = {
            (0, 0, 0): base,
            (1, 0, 0): px, (-1, 0, 0): mx, (0, 1, 0): py, (0, -1, 0): my,
            (0, 0, 1): base + dz, (0, 0, -1): base - dz,
            (1, 1, 0): px + dy, (1, -1, 0): px - dy, (-1, 1, 0): mx + dy, (-1, -1, 0): mx - dy,
            (1, 0, 1): px + dz, (1, 0, -1): px - dz, (-1, 0, 1): mx + dz, (-1, 0, -1): mx - dz,
            (0, 1, 1): py + dz, (0, 1, -1): py - dz, (0, -1, 1): my + dz, (0, -1, -1): my - dz,
        }
        fresh = []
        for k in range(19):
            value = jnp.where(solid, p[OPPOSITE[k]], keep * p[k] + terms[VELOCITIES[k]])
            fresh.append(value)
            emit(k, value)
        return fresh

    loads[0].wait()
    for k in ORDER:
        for t in range(tiles):
            adj[0, PLACE[k], t, own, :] = seed[k, :, pl.ds(t * LANES, LANES)]
    pack(0, 0, lambda k: seed[k, :, pl.ds(0, LANES)])
    pack(0, 1, lambda k: seed[k, :, pl.ds((tiles - 1) * LANES, LANES)])
    pl.semaphore_wait(barrier, 8)
    moves = transfers(0)
    for move in moves:
        move.start()

    for load in loads[1:]:
        load.wait()
    for t in range(tiles):
        cols = pl.ds(t * LANES, LANES)
        rate_ref[:, cols] = (
            OMEGA_BASE + OMEGA_SPAN * field_ref[:, cols] * mask_ref[:, cols].astype(jnp.float32)
        )
    sent = []
    stores = []
    for n in range(steps):
        s = steps - 1 - n
        saved_loads[s].wait()
        prepare(s)
        for move in moves:
            move.wait_recv()
        sent += moves
        last = n == steps - 1
        edge_tiles = [0] if tiles == 1 else [0, tiles - 1]
        for t in edge_tiles + list(range(1, tiles - 1)):
            cols = pl.ds(t * LANES, LANES)
            if last:
                def emit(k, value):
                    out[k, :, cols] = value
            else:
                def emit(k, value):
                    adj[n + 1, PLACE[k], t, own, :] = value
            fresh = advance(n, t, emit)
            if last:
                store = pltpu.make_async_copy(out.at[:, :, cols], out_hbm.at[:, :, cols], out_sem.at[t])
                store.start()
                stores.append(store)
                continue
            if t == 0:
                pack(n + 1, 0, lambda k: fresh[k])
            if t == tiles - 1:
                pack(n + 1, 1, lambda k: fresh[k])
            if t == edge_tiles[-1]:
                moves = transfers(n + 1)
                for move in moves[2:]:
                    move.start()
        if not last:
            for move in moves[:2]:
                move.start()
    store = pltpu.make_async_copy(sens, sens_hbm, out_sem.at[tiles])
    store.start()
    stores.append(store)
    for move in sent:
        move.wait_send()
    for store in stores:
        store.wait()


def solution(mesh):
    num_x, num_y = mesh.shape["gx"], mesh.shape["gy"]

    def body(saved_pops, seed_adjoint, solid_label, design_mask, design_field):
        steps = saved_pops.shape[0]
        width, flat = seed_adjoint.shape[1:]
        tiles = flat // LANES
        rows = 2 * TOP + width
        f32 = jnp.float32
        whole = pl.BlockSpec(memory_space=pl.ANY)
        return pl.pallas_call(
            functools.partial(kernel, num_x, num_y, steps, width, flat),
            out_shape=(
                jax.ShapeDtypeStruct((19, width, flat), f32),
                jax.ShapeDtypeStruct((width, flat), f32),
            ),
            in_specs=[whole] * 5,
            out_specs=(whole, whole),
            scratch_shapes=[
                pltpu.VMEM((steps, 19, width, flat), saved_pops.dtype),
                pltpu.VMEM((19, width, flat), f32),
                pltpu.VMEM((width, flat), jnp.int32),
                pltpu.VMEM((width, flat), jnp.int32),
                pltpu.VMEM((width, flat), f32),
                pltpu.VMEM((steps, 19, tiles, rows, LANES), f32),
                pltpu.VMEM((steps, 2, 2, rows, LANES), f32),
                pltpu.VMEM((steps, 2, 2, rows, LANES), f32),
                pltpu.VMEM((steps, 4, tiles, width, LANES), f32),
                pltpu.VMEM((width, flat), f32),
                pltpu.VMEM((19, width, flat), f32),
                pltpu.VMEM((width, flat), f32),
                pltpu.SemaphoreType.DMA((4,)),
                pltpu.SemaphoreType.DMA((steps,)),
                pltpu.SemaphoreType.DMA((tiles + 1,)),
                pltpu.SemaphoreType.DMA((steps, 8)),
                pltpu.SemaphoreType.DMA((steps, 8)),
            ],
            compiler_params=pltpu.CompilerParams(
                collective_id=0, has_side_effects=True, vmem_limit_bytes=40 * 1024 * 1024
            ),
        )(saved_pops, seed_adjoint, solid_label, design_mask, design_field)

    in_specs = (
        P(None, None, "gx", "gy"),
        P(None, "gx", "gy"),
        P("gx", "gy"),
        P("gx", "gy"),
        P("gx", "gy"),
    )
    out_specs = (P(None, "gx", "gy"), P("gx", "gy"))
    return jax.shard_map(body, mesh=mesh, in_specs=in_specs, out_specs=out_specs, check_vma=False)
```

time: 161 us -> 32.2 us (0.20); the launches traced: 157 us -> 31.8 us
  local copies, waits for them, and re-layouts: 37.4 us -> 6.08 us
  waiting for transfers between devices: 30.8 us -> 0 us
  other arithmetic: 30.5 us -> 0 us
  starting transfers between devices: 29 us -> 0 us
  matrix products: 27 us -> 0 us
  Pallas kernels: 0 us -> 25 us
  between operations: 2.8 us -> 0.65 us
    ppermute x16 -> x0, waiting for transfers between devices: 30.8 us -> none  [the longest x8 21.3 us: extended(): lax.ppermute(tail, axis, [(i, (i + 1) % count) for i in range(count)])]
    ppermute x16 -> x0, starting transfers between devices: 29 us -> none  [the longest x8 22.6 us: extended(): lax.ppermute(head, axis, [((i + 1) % count, i) for i in range(count)])]
    dot_general x16 -> x0, matrix products: 27 us -> none  [the longest x8 14.4 us: collide(): jnp.tensordot(velo, speed, axes=1, precision=lax.Precision.HIGHEST)]
    pallas_call x0 -> x1, Pallas kernels: none -> 25 us  [body(): pl.pallas_call(functools.partial(kernel, num_x, num_y, steps, width, flat...]
    reshape x8 -> x0, local copies, waits for them, and re-layouts: 16.5 us -> none  [the longest x4 12.9 us: padded_field(): return padded.reshape(19, width + 2, (rows + 2) * depth)]
    concatenate x44 -> x0, other arithmetic: 14.4 us -> none  [the longest x4 11.3 us: extended(): jnp.concatenate([lax.ppermute(tail, axis, [(i, (i + 1) % count) for i in...]
    scatter-add x4 -> x0, other arithmetic: 8.51 us -> none  [collide(): bounce = pops[OPPOSITE]]
    slice x70 -> x0, local copies, waits for them, and re-layouts: 7.3 us -> none  [the longest x1 2.07 us: body(): pops = saved_pops[step].astype(jnp.float32) * weights]
  transfers between devices with their start and end apart: 16 -> 0, of which waited for: 10 -> 0; matrix products, arithmetic and copies ran while one was open for 10% -> 0% of each run, Pallas kernels for 0% -> 0%
where the time goes in v1:
time: 32.2 us; the launch traced here: 31.8 us
  Pallas kernels  25 us (78%)
  local copies, waits for them, and re-layouts  6.08 us (19%)
  between operations  0.65 us (2%)
    pallas_call x1, Pallas kernels, body(): pl.pallas_call(functools.partial(kernel, num_x, num_y, steps, width, flat...  25 us
    unnamed x12, local copies, waits for them, and re-layouts  6.08 us

profile of v1, /device:TPU:0, one launch (start us, length us, event | category | flops | bytes accessed | tf_op | source)
XLA Modules:
  0.0 31.8 jit_solution(6938503135067109319)
XLA Ops:
  0.6 0.0 copy-start
  0.6 1.3 %copy-done = bf16[4,19,16,512]{3,2,1,0:T(8,128)(2,1)S(1)} copy-done((bf16[4,19,16,512]{3,2,1,0:T(8,128)(2,1)S(1)}, bf16[4,19,16,512]{3,2,1,0:T(8,128)(2,1)}, u32[]{:S(2)}) %copy-start) | copy-done | bytes 1245208
  1.9 0.0 copy-start.1
  1.9 1.1 %copy-done.1 = f32[19,16,512]{2,1,0:T(8,128)S(1)} copy-done((f32[19,16,512]{2,1,0:T(8,128)S(1)}, f32[19,16,512]{2,1,0:T(8,128)}, u32[]{:S(2)}) %copy-start.1) | copy-done | bytes 622616
  3.0 0.0 copy-start.2
  3.0 0.8 %copy-done.2 = s32[16,512]{1,0:T(8,128)S(1)} copy-done((s32[16,512]{1,0:T(8,128)S(1)}, s32[16,512]{1,0:T(8,128)}, u32[]{:S(2)}) %copy-start.2) | copy-done | bytes 32792
  3.8 0.0 copy-start.3
  3.8 0.8 %copy-done.3 = s32[16,512]{1,0:T(8,128)S(1)} copy-done((s32[16,512]{1,0:T(8,128)S(1)}, s32[16,512]{1,0:T(8,128)}, u32[]{:S(2)}) %copy-start.3) | copy-done | bytes 32792
  4.5 0.0 copy-start.4
  4.5 0.8 %copy-done.4 = f32[16,512]{1,0:T(8,128)S(1)} copy-done((f32[16,512]{1,0:T(8,128)S(1)}, f32[16,512]{1,0:T(8,128)}, u32[]{:S(2)}) %copy-start.4) | copy-done | bytes 32792
  5.3 25.0 %shard_map.68 = (f32[19,16,512]{2,1,0:T(8,128)S(1)}, f32[16,512]{1,0:T(8,128)S(1)}) custom-call(bf16[4,19,16,512]{3,2,1,0:T(8,128)(2,1)S(1)} %copy-done, f32[19,16,512]{2,1,0:T(8,128)S(1)} %copy-done.1, s32[16,512]{1,0:T(8,128)S(1)} %copy-done.2, s32[16,512]{1,0:T(8,128)S(1)} %copy-done.3, f32[16,512]{1,0:T(8,128)S(1)} %copy-done.4), custom_call_target="tpu_custom_call" | custom-call | tf_op jit(solution)/shard_map/pallas_call | solution.py:298
  30.3 0.8 %copy.9 = f32[19,16,512]{2,1,0:T(8,128)} copy(f32[19,16,512]{2,1,0:T(8,128)S(1)} %get-tuple-element.4) | data formatting | bytes 1245184
  31.2 0.6 %copy.10 = f32[16,512]{1,0:T(8,128)} copy(f32[16,512]{1,0:T(8,128)S(1)} %get-tuple-element.5) | data formatting | bytes 65536
Async XLA Ops:
  0.6 1.3 %copy-start = (bf16[4,19,16,512]{3,2,1,0:T(8,128)(2,1)S(1)}, bf16[4,19,16,512]{3,2,1,0:T(8,128)(2,1)}, u32[]{:S(2)}) copy-start(bf16[4,19,16,512]{3,2,1,0:T(8,128)(2,1)} %saved_hbm.1) | copy-start | bytes 3735556
  1.9 1.1 %copy-start.1 = (f32[19,16,512]{2,1,0:T(8,128)S(1)}, f32[19,16,512]{2,1,0:T(8,128)}, u32[]{:S(2)}) copy-start(f32[19,16,512]{2,1,0:T(8,128)} %seed_hbm.1) | copy-start | bytes 1867780
  3.0 0.8 %copy-start.2 = (s32[16,512]{1,0:T(8,128)S(1)}, s32[16,512]{1,0:T(8,128)}, u32[]{:S(2)}) copy-start(s32[16,512]{1,0:T(8,128)} %solid_hbm.1) | copy-start | bytes 98308
  3.8 0.8 %copy-start.3 = (s32[16,512]{1,0:T(8,128)S(1)}, s32[16,512]{1,0:T(8,128)}, u32[]{:S(2)}) copy-start(s32[16,512]{1,0:T(8,128)} %mask_hbm.1) | copy-start | bytes 98308
  4.5 0.8 %copy-start.4 = (f32[16,512]{1,0:T(8,128)S(1)}, f32[16,512]{1,0:T(8,128)}, u32[]{:S(2)}) copy-start(f32[16,512]{1,0:T(8,128)} %field_hbm.1) | copy-start | bytes 98308

commit v2 on v1

v2 whole, which is shorter than its diff:
```python
import functools

import jax
import jax.numpy as jnp
import numpy as np
from jax import lax
from jax.experimental import pallas as pl
from jax.experimental.pallas import tpu as pltpu
from jax.sharding import PartitionSpec as P

NZ = 32
LANES = 128
MESH = pl.DeviceIdType.MESH

VELOCITIES = [
    (0, 0, 0),
    (1, 0, 0), (-1, 0, 0), (0, 1, 0), (0, -1, 0), (0, 0, 1), (0, 0, -1),
    (1, 1, 0), (1, -1, 0), (-1, 1, 0), (-1, -1, 0),
    (1, 0, 1), (1, 0, -1), (-1, 0, 1), (-1, 0, -1),
    (0, 1, 1), (0, 1, -1), (0, -1, 1), (0, -1, -1),
]
OPPOSITE = [0, 2, 1, 4, 3, 6, 5, 10, 9, 8, 7, 14, 13, 12, 11, 18, 17, 16, 15]
OMEGA_BASE = 1.0
OMEGA_SPAN = 0.8
SENS_SCALE = 10.0

EXTRA_ROWS = 8
WIDTH_SENT = 2


def roll_lanes(value, shift):
    shift = shift % LANES
    return value if shift == 0 else pltpu.roll(value, shift, 1)


def kernel(
    num_x, num_y, steps, width, flat,
    saved_hbm, seed_hbm, solid_hbm, mask_hbm, field_hbm,
    out_hbm, sens_hbm,
    saved, solid_ref, mask_ref, field_ref,
    adj, xsend, xrecv, ysend, yrecv, density_ref, speed, mark, out, sens,
    in_sem, seed_sem, saved_sem, out_sem, send_sem, recv_sem,
):
    tiles = flat // LANES
    ring = width + EXTRA_ROWS
    half = LANES // 2
    gx, gy = lax.axis_index("gx"), lax.axis_index("gy")
    west, east = lax.rem(gx + num_x - 1, num_x), lax.rem(gx + 1, num_x)
    south, north = lax.rem(gy + num_y - 1, num_y), lax.rem(gy + 1, num_y)

    barrier = pltpu.get_barrier_semaphore()
    around = [
        (west, south), (east, south), (west, north), (east, north),
        (west, gy), (east, gy), (gx, south), (gx, north),
    ]
    for device in around:
        pl.semaphore_signal(barrier, inc=1, device_id=device, device_id_type=MESH)
    own = pl.ds(0, width)

    def columns(t):
        return pl.ds(t * LANES, LANES)

    loads = [
        pltpu.make_async_copy(solid_hbm, solid_ref, in_sem.at[0]),
        pltpu.make_async_copy(mask_hbm, mask_ref, in_sem.at[1]),
        pltpu.make_async_copy(field_hbm, field_ref, in_sem.at[2]),
    ]
    seed_loads = [
        pltpu.make_async_copy(seed_hbm.at[:, :, columns(t)], adj.at[0, :, t, own], seed_sem.at[t])
        for t in range(tiles)
    ]
    saved_loads = [
        pltpu.make_async_copy(saved_hbm.at[steps - 1 - n], saved.at[steps - 1 - n], saved_sem.at[n])
        for n in range(steps)
    ]
    ahead = list(range(0, steps, 2))
    for n in ahead:
        saved_loads[n].start()
    for load in loads + seed_loads:
        load.start()
    for n in range(1, steps, 2):
        saved_loads[n].start()

    lane = lax.broadcasted_iota(jnp.int32, (ring, LANES), 1)
    depth = lane % NZ

    def view(n, item):
        if isinstance(item, int):
            return adj.at[n, item]
        return mark.at[item[1]] if item[0] == "mark" else speed.at[item[1], item[2]]

    def plan(n):
        fields = []
        if n == 0:
            fields = [("speed", m, axis) for m in ahead if m + 1 < steps for axis in range(3)]
            fields += [("mark", 0), ("mark", 1)]
        rows, packs = [], []
        for sign in (1, -1):
            near, next_one = (0, 1) if sign == 1 else (width - 1, width - 2)
            rows.append(
                [(k, near) for k in range(19) if VELOCITIES[k][0] * sign >= 0]
                + [(k, next_one) for k in range(19) if VELOCITIES[k][0] * sign > 0]
                + [(field, near) for field in fields]
            )
            packs.append([k for k in range(19) if VELOCITIES[k][1] * sign >= 0] + fields)
        return rows, packs

    def place(row):
        return width + row if row < WIDTH_SENT else ring - width + row

    def transfers(n):
        pair = n // 2
        rows, packs = plan(n)
        moves = []

        def add(src, dst, device):
            i = len(moves)
            moves.append(
                pltpu.make_async_remote_copy(
                    src_ref=src, dst_ref=dst,
                    send_sem=send_sem.at[pair, i], recv_sem=recv_sem.at[pair, i],
                    device_id=device, device_id_type=MESH,
                )
            )

        for side, by_x in ((0, (west, east)), (1, (west, east))):
            by_y = (south, north)[side]
            count = pl.ds(0, (len(packs[side]) + 1) // 2)
            for x, src_row, dst_row in (
                (by_x[0], 0, width), (by_x[1], width - WIDTH_SENT, ring - WIDTH_SENT),
            ):
                add(
                    ysend.at[pair, side, count, pl.ds(src_row, WIDTH_SENT)],
                    yrecv.at[pair, side, count, pl.ds(dst_row, WIDTH_SENT)],
                    (x, by_y),
                )
        for side, by_y in ((0, south), (1, north)):
            count = pl.ds(0, (len(packs[side]) + 1) // 2)
            add(ysend.at[pair, side, count, own], yrecv.at[pair, side, count, own], (gx, by_y))
        for side, by_x in ((0, west), (1, east)):
            count = pl.ds(0, len(rows[side]) * tiles)
            add(xsend.at[pair, side, count], xrecv.at[pair, side, count], (by_x, gy))
        return moves

    def first_half(side):
        return (lane < half) if side == 0 else (lane >= half)

    def pack_y(n, side):
        pack = plan(n)[1][side]
        t = 0 if side == 0 else tiles - 1
        for i in range(0, len(pack), 2):
            value = view(n, pack[i])[t, own, :]
            if i + 1 < len(pack):
                second = roll_lanes(view(n, pack[i + 1])[t, own, :], half)
                value = jnp.where(first_half(side)[:width], value, second)
            ysend[n // 2, side, i // 2, own, :] = value

    def pack_x(n):
        for side, rows in enumerate(plan(n)[0]):
            for j, (item, row) in enumerate(rows):
                for t in range(tiles):
                    xsend[n // 2, side, pl.ds(j * tiles + t, 1), :] = view(n, item)[t, pl.ds(row, 1), :]

    def unpack(n):
        rows, packs = plan(n)
        for side in range(2):
            for j, (item, row) in enumerate(rows[side]):
                for t in range(tiles):
                    view(n, item)[t, pl.ds(place(row), 1), :] = xrecv[
                        n // 2, side, pl.ds(j * tiles + t, 1), :
                    ]

        def arrived(side, item):
            if item not in packs[side]:
                return None
            i = packs[side].index(item)
            return roll_lanes(yrecv[n // 2, side, i // 2], half * (i % 2))

        for item in packs[0] + [item for item in packs[1] if item not in packs[0]]:
            after, before = arrived(0, item), arrived(1, item)
            if after is None or before is None:
                value = before if after is None else after
            else:
                value = jnp.where(lane < half, after, before)
            view(n, item)[tiles] = value

    def pulled_tile(n, k, t, count):
        step_x, step_y, step_z = VELOCITIES[k]
        if step_x == 0:
            rows = pl.ds(0, count)
        elif step_x == 1 and count == width:
            rows, step_x = pl.ds(1, count), 0
        else:
            rows = pl.ds(0, ring)
        value = adj[n, k, t, rows, :]
        if step_y != 0:
            beside = adj[n, k, (t + step_y) % (tiles + 1), rows, :]
            at = lane[: value.shape[0]]
            value = jnp.where(at < NZ if step_y == 1 else at >= LANES - NZ, beside, value)
        if step_x != 0:
            value = pltpu.roll(value, (-step_x) % ring, 0)[:count]
        shift = -NZ * step_y
        if step_z == 0:
            return roll_lanes(value, shift)
        return jnp.where(
            depth[:count] == (NZ - 1 if step_z == 1 else 0),
            roll_lanes(value, shift - step_z + NZ * step_z),
            roll_lanes(value, shift - step_z),
        )

    def moments(v):
        xy_a, xy_b, xy_c, xy_d = v(7) + v(8), v(9) + v(10), v(7) - v(8), v(9) - v(10)
        xz_a, xz_b, xz_c, xz_d = v(11) + v(12), v(13) + v(14), v(11) - v(12), v(13) - v(14)
        yz_a, yz_b, yz_c, yz_d = v(15) + v(16), v(17) + v(18), v(15) - v(16), v(17) - v(18)
        xy, xz, yz = xy_a + xy_b, xz_a + xz_b, yz_a + yz_b
        face_x, face_y, face_z = 2.0 * (v(1) + v(2)), 2.0 * (v(3) + v(4)), 2.0 * (v(5) + v(6))
        total = 12.0 * v(0) + (face_x + face_y + face_z) + (xy + xz + yz)
        first = (
            2.0 * (v(1) - v(2)) + (xy_a - xy_b) + (xz_a - xz_b),
            2.0 * (v(3) - v(4)) + (xy_c + xy_d) + (yz_a - yz_b),
            2.0 * (v(5) - v(6)) + (xz_c + xz_d) + (yz_c + yz_d),
        )
        second = (
            face_x + xy + xz, face_y + xy + yz, face_z + xz + yz,
            xy_c - xy_d, xz_c - xz_d, yz_c - yz_d,
        )
        return total, first, second

    def prepare(n):
        saved_loads[n].wait()
        for t in range(tiles):
            pops = [saved[steps - 1 - n, k, :, columns(t)].astype(jnp.float32) for k in range(19)]
            total, first, unused = moments(lambda k: pops[k])
            inverse = 1.0 / total
            density_ref[n, t] = total
            for axis in range(3):
                speed[n, axis, t, own, :] = first[axis] * inverse

    def advance(n, t, count, emit):
        s = steps - 1 - n
        cols = columns(t)
        rows = pl.ds(0, count)
        p = [pulled_tile(n, k, t, count) for k in range(19)]
        total, first, second = moments(lambda k: p[k])
        ux, uy, uz = (speed[n, axis, t, rows, :] for axis in range(3))
        xx, yy, zz, xy, xz, yz = (0.25 * value for value in second)
        gx_, gy_, gz_ = (value * (1.0 / 12.0) for value in first)
        total3 = total * (1.0 / 12.0)
        dx = gx_ + (xx - total3) * ux + xy * uy + xz * uz
        dy = gy_ + (yy - total3) * uy + xy * ux + yz * uz
        dz = gz_ + (zz - total3) * uz + xz * ux + yz * uy
        half_g = 0.5 * (gx_ * ux + gy_ * uy + gz_ * uz)
        half_d = 0.5 * (dx * ux + dy * uy + dz * uz)
        base = total * (1.0 / 36.0) + half_g
        solid = mark[1, t, rows, :] > 0.5
        if t < tiles:
            prod = [p[k][:width] * saved[s, k, :, cols].astype(jnp.float32) for k in range(19)]
            faces = (prod[1] + prod[2]) + (prod[3] + prod[4]) + (prod[5] + prod[6])
            edges = ((prod[7] + prod[8]) + (prod[9] + prod[10])) + (
                (prod[11] + prod[12]) + (prod[13] + prod[14])
            )
            edges = edges + ((prod[15] + prod[16]) + (prod[17] + prod[18]))
            gain = density_ref[n, t] * (base + half_d)[:width] - (12.0 * prod[0] + 2.0 * faces + edges)
            sens_now = gain if n == 0 else sens[:, cols] + gain
            if n == steps - 1:
                factor = mask_ref[:, cols].astype(jnp.float32) * (SENS_SCALE * OMEGA_SPAN / 36.0)
                sens_now = jnp.where(solid[:width], 0.0, factor * sens_now)
            sens[:, cols] = sens_now
        rate = mark[0, t, rows, :]
        keep = 1.0 - rate
        base = rate * (base - half_d)
        dx, dy, dz = rate * dx, rate * dy, rate * dz
        px, mx = base + dx, base - dx
        py, my = base + dy, base - dy
        terms = {
            (0, 0, 0): base,
            (1, 0, 0): px, (-1, 0, 0): mx, (0, 1, 0): py, (0, -1, 0): my,
            (0, 0, 1): base + dz, (0, 0, -1): base - dz,
            (1, 1, 0): px + dy, (1, -1, 0): px - dy, (-1, 1, 0): mx + dy, (-1, -1, 0): mx - dy,
            (1, 0, 1): px + dz, (1, 0, -1): px - dz, (-1, 0, 1): mx + dz, (-1, 0, -1): mx - dz,
            (0, 1, 1): py + dz, (0, 1, -1): py - dz, (0, -1, 1): my + dz, (0, -1, -1): my - dz,
        }
        for k in range(19):
            if t == tiles and VELOCITIES[k][1] == 0:
                continue
            some = count if VELOCITIES[k][0] != 0 else width
            emit(
                k, some,
                jnp.where(
                    solid[:some], p[OPPOSITE[k]][:some],
                    keep[:some] * p[k][:some] + terms[VELOCITIES[k]][:some],
                ),
            )

    for load in loads:
        load.wait()
    for t in range(tiles):
        cols = columns(t)
        mark[0, t, own, :] = (
            OMEGA_BASE + OMEGA_SPAN * field_ref[:, cols] * mask_ref[:, cols].astype(jnp.float32)
        )
        mark[1, t, own, :] = (solid_ref[:, cols] > 0).astype(jnp.float32)
    for n in ahead:
        prepare(n)
    for load in seed_loads:
        load.wait()

    sent, stores = [], []
    for n in range(steps):
        if n % 2 == 0:
            for side in range(2):
                pack_y(n, side)
            if n == 0:
                pl.semaphore_wait(barrier, len(around))
            moves = transfers(n)
            for move in moves[:6]:
                move.start()
            pack_x(n)
            for move in moves[6:]:
                move.start()
            sent += moves
            if n + 1 < steps:
                prepare(n + 1)
            for move in reversed(moves):
                move.wait_recv()
            unpack(n)
        last = n == steps - 1
        beyond = n % 2 == 0 and not last
        for t in range(tiles + 1 if beyond else tiles):
            cols = columns(t)
            if last:
                def emit(k, some, value):
                    out[k, :, cols] = value
            else:
                def emit(k, some, value):
                    adj[n + 1, k, t, pl.ds(0, some), :] = value
            advance(n, t, ring if beyond else width, emit)
            if last:
                store = pltpu.make_async_copy(out.at[:, :, cols], out_hbm.at[:, :, cols], out_sem.at[t])
                store.start()
                stores.append(store)
    store = pltpu.make_async_copy(sens, sens_hbm, out_sem.at[tiles])
    store.start()
    stores.append(store)
    for move in sent:
        move.wait_send()
    for store in stores:
        store.wait()


def solution(mesh):
    num_x, num_y = mesh.shape["gx"], mesh.shape["gy"]

    def body(saved_pops, seed_adjoint, solid_label, design_mask, design_field):
        steps = saved_pops.shape[0]
        width, flat = seed_adjoint.shape[1:]
        tiles = flat // LANES
        ring = width + EXTRA_ROWS
        pairs = (steps + 1) // 2
        fields = 3 * (steps // 2) + 2
        row_items = 19 + fields
        packs = (14 + fields + 1) // 2
        f32 = jnp.float32
        whole = pl.BlockSpec(memory_space=pltpu.HBM)
        return pl.pallas_call(
            functools.partial(kernel, num_x, num_y, steps, width, flat),
            out_shape=(
                jax.ShapeDtypeStruct((19, width, flat), f32),
                jax.ShapeDtypeStruct((width, flat), f32),
            ),
            in_specs=[whole] * 5,
            out_specs=(whole, whole),
            scratch_shapes=[
                pltpu.VMEM((steps, 19, width, flat), saved_pops.dtype),
                pltpu.VMEM((width, flat), jnp.int32),
                pltpu.VMEM((width, flat), jnp.int32),
                pltpu.VMEM((width, flat), f32),
                pltpu.VMEM((steps, 19, tiles + 1, ring, LANES), f32),
                pltpu.VMEM((pairs, 2, row_items * tiles, LANES), f32),
                pltpu.VMEM((pairs, 2, row_items * tiles, LANES), f32),
                pltpu.VMEM((pairs, 2, packs, ring, LANES), f32),
                pltpu.VMEM((pairs, 2, packs, ring, LANES), f32),
                pltpu.VMEM((steps, tiles, width, LANES), f32),
                pltpu.VMEM((steps, 3, tiles + 1, ring, LANES), f32),
                pltpu.VMEM((2, tiles + 1, ring, LANES), f32),
                pltpu.VMEM((19, width, flat), f32),
                pltpu.VMEM((width, flat), f32),
                pltpu.SemaphoreType.DMA((3,)),
                pltpu.SemaphoreType.DMA((tiles,)),
                pltpu.SemaphoreType.DMA((steps,)),
                pltpu.SemaphoreType.DMA((tiles + 1,)),
                pltpu.SemaphoreType.DMA((pairs, 8)),
                pltpu.SemaphoreType.DMA((pairs, 8)),
            ],
            compiler_params=pltpu.CompilerParams(
                collective_id=0, has_side_effects=True, vmem_limit_bytes=62 * 1024 * 1024
            ),
        )(saved_pops, seed_adjoint, solid_label, design_mask, design_field)

    in_specs = (
        P(None, None, "gx", "gy"),
        P(None, "gx", "gy"),
        P("gx", "gy"),
        P("gx", "gy"),
        P("gx", "gy"),
    )
    out_specs = (P(None, "gx", "gy"), P("gx", "gy"))
    return jax.shard_map(body, mesh=mesh, in_specs=in_specs, out_specs=out_specs, check_vma=False)
```

time: 32.2 us -> 23 us (0.71)
  Pallas kernels: 25 us -> 19.6 us
  local copies, waits for them, and re-layouts: 6.08 us -> 2.58 us
    pallas_call x1, Pallas kernels: 25 us -> 19.6 us  [body(): pl.pallas_call(functools.partial(kernel, num_x, num_y, steps, width, flat...]
    unnamed x12 -> x4, local copies, waits for them, and re-layouts: 6.08 us -> 2.58 us
where the time goes in v2:
time: 23 us; the launch traced here: 22.9 us
  Pallas kernels  19.6 us (85%)
  local copies, waits for them, and re-layouts  2.58 us (11%)
  between operations  0.65 us (3%)
    pallas_call x1, Pallas kernels, body(): pl.pallas_call(functools.partial(kernel, num_x, num_y, steps, width, flat...  19.6 us
    unnamed x4, local copies, waits for them, and re-layouts  2.58 us

profile of v2, /device:TPU:0, one launch (start us, length us, event | category | flops | bytes accessed | tf_op | source)
XLA Modules:
  0.0 22.9 jit_solution(14566434844094898618)
XLA Ops:
  0.6 19.6 %shard_map.68 = (f32[19,16,512]{2,1,0:T(8,128)}, f32[16,512]{1,0:T(8,128)}) custom-call(bf16[4,19,16,512]{3,2,1,0:T(8,128)(2,1)} %saved_hbm.1, f32[19,16,512]{2,1,0:T(8,128)} %seed_hbm.1, s32[16,512]{1,0:T(8,128)} %solid_hbm.1, s32[16,512]{1,0:T(8,128)} %mask_hbm.1, f32[16,512]{1,0:T(8,128)} %field_hbm.1), custom_call_target="tpu_custom_call" | custom-call | tf_op jit(solution)/shard_map/pallas_call | solution.py:365
  20.3 0.0 copy-start
  20.3 2.0 %copy.9 = f32[19,16,512]{2,1,0:T(8,128)} copy(f32[19,16,512]{2,1,0:T(8,128)} %get-tuple-element.4) | data formatting | bytes 1245184
  22.3 0.0 copy-done
  22.3 0.6 %copy.10 = f32[16,512]{1,0:T(8,128)} copy(f32[16,512]{1,0:T(8,128)S(1)} %copy-done) | data formatting | bytes 65536
Async XLA Ops:
  20.3 2.0 %copy-start = (f32[16,512]{1,0:T(8,128)S(1)}, f32[16,512]{1,0:T(8,128)}, u32[]{:S(2)}) copy-start(f32[16,512]{1,0:T(8,128)} %get-tuple-element.5) | copy-start | bytes 98308

commit v3 on v2

--- a/solution.py
+++ b/solution.py
@@ -348,6 +348,22 @@
         store.wait()
 
 
+def hand_over(out_from, sens_from, out_to, sens_to, out, sens, in_sem, out_sem):
+    parts = [(sens_from, sens, sens_to)]
+    for first, last in ((0, 5), (5, 10), (10, 15), (15, 19)):
+        part = pl.ds(first, last - first)
+        parts.append((out_from.at[part], out.at[part], out_to.at[part]))
+    loads = [pltpu.make_async_copy(a, b, in_sem.at[i]) for i, (a, b, c) in enumerate(parts)]
+    stores = [pltpu.make_async_copy(b, c, out_sem.at[i]) for i, (a, b, c) in enumerate(parts)]
+    for load in loads:
+        load.start()
+    for load, store in zip(loads, stores):
+        load.wait()
+        store.start()
+    for store in stores:
+        store.wait()
+
+
 def solution(mesh):
     num_x, num_y = mesh.shape["gx"], mesh.shape["gy"]
 
@@ -362,7 +378,7 @@
         packs = (14 + fields + 1) // 2
         f32 = jnp.float32
         whole = pl.BlockSpec(memory_space=pltpu.HBM)
-        return pl.pallas_call(
+        results = pl.pallas_call(
             functools.partial(kernel, num_x, num_y, steps, width, flat),
             out_shape=(
                 jax.ShapeDtypeStruct((19, width, flat), f32),
@@ -396,6 +412,22 @@
                 collective_id=0, has_side_effects=True, vmem_limit_bytes=62 * 1024 * 1024
             ),
         )(saved_pops, seed_adjoint, solid_label, design_mask, design_field)
+        return pl.pallas_call(
+            hand_over,
+            out_shape=(
+                jax.ShapeDtypeStruct((19, width, flat), f32),
+                jax.ShapeDtypeStruct((width, flat), f32),
+            ),
+            in_specs=[whole] * 2,
+            out_specs=(whole, whole),
+            scratch_shapes=[
+                pltpu.VMEM((19, width, flat), f32),
+                pltpu.VMEM((width, flat), f32),
+                pltpu.SemaphoreType.DMA((5,)),
+                pltpu.SemaphoreType.DMA((5,)),
+            ],
+            compiler_params=pltpu.CompilerParams(vmem_limit_bytes=62 * 1024 * 1024),
+        )(*results)
 
     in_specs = (
         P(None, None, "gx", "gy"),

time: 23 us -> 22.4 us (0.974)
  local copies, waits for them, and re-layouts: 2.58 us -> 0 us
  Pallas kernels: 19.6 us -> 21.5 us
    unnamed x4 -> x0, local copies, waits for them, and re-layouts: 2.58 us -> none
    pallas_call x0 -> x1, Pallas kernels: none -> 1.9 us  [body(): pl.pallas_call(hand_over, out_shape=(jax.ShapeDtypeStruct((19, width, fla...]
where the time goes in v3:
time: 22.4 us; the launch traced here: 22.2 us
  Pallas kernels  21.5 us (96%)
  between operations  0.64 us (3%)
    pallas_call x1, Pallas kernels, body(): pl.pallas_call(functools.partial(kernel, num_x, num_y, steps, width, flat...  19.6 us
    pallas_call x1, Pallas kernels, body(): pl.pallas_call(hand_over, out_shape=(jax.ShapeDtypeStruct((19, width, fla...  1.9 us

profile of v3, /device:TPU:0, one launch (start us, length us, event | category | flops | bytes accessed | tf_op | source)
XLA Modules:
  0.0 22.2 jit_solution(1459458377316444333)
XLA Ops:
  0.6 19.6 %shard_map.68 = (f32[19,16,512]{2,1,0:T(8,128)}, f32[16,512]{1,0:T(8,128)}) custom-call(bf16[4,19,16,512]{3,2,1,0:T(8,128)(2,1)} %saved_hbm.1, f32[19,16,512]{2,1,0:T(8,128)} %seed_hbm.1, s32[16,512]{1,0:T(8,128)} %solid_hbm.1, s32[16,512]{1,0:T(8,128)} %mask_hbm.1, f32[16,512]{1,0:T(8,128)} %field_hbm.1), custom_call_target="tpu_custom_call" | custom-call | tf_op jit(solution)/shard_map/pallas_call | solution.py:381
  20.3 1.9 %shard_map.69 = (f32[19,16,512]{2,1,0:T(8,128)}, f32[16,512]{1,0:T(8,128)}) custom-call(f32[19,16,512]{2,1,0:T(8,128)} %get-tuple-element.4.out_from, f32[16,512]{1,0:T(8,128)} %get-tuple-element.5.sens_from), custom_call_target="tpu_custom_call" | custom-call | tf_op jit(solution)/shard_map/pallas_call | solution.py:415
